TPU v7x, 512 devices: a whole 4x8x8 slice. The times are simulated.
512 devices in a mesh: tm: 128 (over z, y, core), swath: 4 (over x).
Axes of the slice: x: 4, y: 8, z: 8, core: 2. Of those that a mesh axis runs over, the one named last changes fastest.
Arguments:
- design: bfloat16 [128, 2048, 512], P('tm', 'swath'), may hold values from -6 to 6
- process: bfloat16 [128, 512, 512], P('tm', 'swath')
- prior_prec: float32 [128, 512], P('tm', 'swath'), may hold values from 0.05 to 0.5
- routes: int32 [128, 16], P('tm', 'swath'), may hold values from -1 to 127, as said below
- counts: int32 [128, 4], P('tm', 'swath'), may hold values from 1 to 4
Outputs:
- reduced_diag: float32 [128, 512, 512], P('tm', 'swath')
- reduced_coupling: float32 [128, 512, 512], P('tm', 'swath')
Inputs may be any that keep to these rules, and one draw needn't show every extreme that they name: `routes`: each value is the holder's own time block i or i + 1, or -1 only where i + 1 would be 128; of one holder's 4 blocks, exactly 2 name i and the others i + 1 or -1.
All inputs are finite; a program needn't handle non-finite values.
Results may differ from a plain program's by a relative error of at most 0.00073.
Values may be sent and summed in bfloat16 or wider, within the bound.
No kernel may reach another device: no remote copies, remote signals or barrier semaphores. Data moves between devices by JAX's collectives and lax.ppermute only.
A program may use at most 64 MiB of HBM per device.

v0:
```python
import jax
import jax.numpy as jnp
from jax import lax
from jax.sharding import PartitionSpec as P

LEVELS = 3


def passed_along(block, axis, distance):
    devices = range(lax.axis_size(axis))
    route = [(i - distance, i) for i in devices if i - distance in devices]
    return lax.ppermute(block, axis, route)


def tri_solve(factor, right):
    return lax.linalg.triangular_solve(factor, right, left_side=True, lower=True)


def inner_rows(left_side, right_side):
    return lax.dot_general(
        left_side,
        right_side,
        (((0,), (0,)), ((), ())),
        precision=lax.Precision.HIGHEST,
        preferred_element_type=jnp.float32,
    )


def compact(scaled, wanted, slot_count):
    sort_key = jnp.where(wanted, 0, 1).astype(jnp.int32)
    picked = jnp.argsort(sort_key, stable=True)[:slot_count]
    kept = jnp.take(sort_key, picked) == 0
    return jnp.where(kept[:, None, None], scaled[picked], 0.0).astype(jnp.bfloat16)


def shards(design, process, prior_prec, routes, counts):
    row_count = process.shape[1]
    order_size = process.shape[2]
    time_count = lax.axis_size("tm")
    my_time = lax.axis_index("tm")
    swath_index = lax.axis_index("swath")
    block_count = routes.shape[1]
    slot_count = block_count // 2
    block_rows = design.shape[1] // block_count
    total_slots = 2 * slot_count * block_rows * lax.axis_size("swath")
    row_start = swath_index * row_count
    raw_rows = design[0].reshape(block_count, block_rows, order_size).astype(jnp.float32)
    mean_sq = jnp.mean(raw_rows * raw_rows, axis=-1, keepdims=True)
    scaled = raw_rows * lax.rsqrt(4.0 * total_slots * (mean_sq + 1e-06))
    live = jnp.arange(block_count) < counts[0, 0]
    target = routes[0]
    own_blocks = compact(scaled, live & (target == my_time), slot_count)
    ahead_blocks = compact(scaled, live & (target == my_time + 1), slot_count)
    incoming, previous = passed_along((ahead_blocks, process), "tm", 1)
    gram_input = jnp.concatenate([own_blocks, incoming], axis=0).reshape(-1, order_size)
    shard_rows = lax.all_gather(gram_input, "swath", axis=0, tiled=True)
    columns = lax.dynamic_slice_in_dim(shard_rows, row_start, row_count, 1)
    gram = lax.dot_general(
        columns, shard_rows, (((0,), (0,)), ((), ())), preferred_element_type=jnp.float32
    )
    unit_rows = jnp.arange(order_size)[None, :] == jnp.arange(row_count)[:, None] + row_start
    diag_rows = previous[0].astype(jnp.float32) + process[0].astype(jnp.float32) + gram
    diag_rows = diag_rows + jnp.where(unit_rows, prior_prec[0][:, None], 0.0)
    coup_rows = -process[0].astype(jnp.float32)
    unit_full = jnp.eye(order_size, dtype=jnp.float32)
    for level in range(LEVELS):
        distance = 2**level
        full_diag, full_coup = (
            lax.all_gather(diag_rows, "swath", axis=0, tiled=True),
            lax.all_gather(coup_rows, "swath", axis=0, tiled=True),
        )
        factor = jnp.linalg.cholesky(full_diag)
        solved = tri_solve(factor, full_coup)
        own_cols = lax.dynamic_slice_in_dim(solved, row_start, row_count, 1)
        eliminated = inner_rows(own_cols, solved)
        left_term = passed_along(eliminated, "tm", distance)
        far_factor, far_solved = passed_along((factor, solved), "tm", -distance)
        has_partner = my_time + distance < time_count
        far_factor = jnp.where(has_partner, far_factor, unit_full)
        cross = tri_solve(far_factor, full_coup.T)
        cross_cols = lax.dynamic_slice_in_dim(cross, row_start, row_count, 1)
        right_term = inner_rows(cross_cols, cross)
        new_coupling = inner_rows(cross_cols, far_solved)
        diag_rows = diag_rows - left_term - jnp.where(has_partner, right_term, 0.0)
        coup_rows = -new_coupling
    return (diag_rows[None], coup_rows[None])


def solution(mesh):
    return jax.shard_map(
        shards,
        mesh=mesh,
        in_specs=(
            P("tm", "swath", None),
            P("tm", "swath", None),
            P("tm", "swath"),
            P("tm", "swath"),
            P("tm", "swath"),
        ),
        out_specs=(P("tm", "swath", None), P("tm", "swath", None)),
        check_vma=False,
    )
```

profile of v0, /device:TPU:16, one launch (start us, length us, event | category | flops | bytes accessed | tf_op | source)
XLA Modules:
  0.0 882.1 jit_solution(11233047935860242572)
XLA Ops:
  28.9 35.5 %all-gather.9.cloned.1.call-done = bf16[2048,512]{1,0:T(8,128)(2,1)} async-done(((bf16[512,512]{1,0:T(8,128)(2,1)}), bf16[2048,512]{1,0:T(8,128)(2,1)}) %all-gather.9.cloned.1.call-update) | async-done | bytes 2097168 | tf_op jit(solution)/shard_map/all_gather | solution.py:56
  68.6 30.6 %all-gather.11.cloned.1.call-done = f32[512,512]{0,1:T(8,128)} async-done(((f32[128,512]{0,1:T(8,128)}), f32[512,512]{0,1:T(8,128)}) %all-gather.11.cloned.1.call-update) | async-done | bytes 1048592 | tf_op jit(solution)/shard_map/all_gather | solution.py:69
  101.1 11.7 %cholesky.374 = f32[128,128]{1,0:T(8,128)S(1)} custom-call(f32[128,128]{1,0:T(8,128)S(1)} %cholesky.586), custom_call_target="Cholesky" | custom-call | tf_op jit(solution)/shard_map/jit(cholesky)/cholesky | solution.py:72
  123.5 11.7 %cholesky.393 = f32[128,128]{1,0:T(8,128)S(1)} custom-call(f32[128,128]{1,0:T(8,128)S(1)} %cholesky.590), custom_call_target="Cholesky" | custom-call | tf_op jit(solution)/shard_map/jit(cholesky)/cholesky | solution.py:72
  146.1 11.7 %cholesky.414 = f32[128,128]{1,0:T(8,128)S(1)} custom-call(f32[128,128]{1,0:T(8,128)S(1)} %cholesky.595), custom_call_target="Cholesky" | custom-call | tf_op jit(solution)/shard_map/jit(cholesky)/cholesky | solution.py:72
  168.3 11.7 %cholesky.431 = f32[128,128]{1,0:T(8,128)S(1)} custom-call(f32[128,128]{1,0:T(8,128)S(1)} %convolution_subtract_fusion.14), custom_call_target="Cholesky" | custom-call | tf_op jit(solution)/shard_map/jit(cholesky)/cholesky | solution.py:72
  193.0 39.3 %custom-call.37 = f32[4,128,128]{1,2,0:T(8,128)S(1)} custom-call(f32[4,128,128]{2,1,0:T(8,128)S(1)} %get-tuple-element.47), custom_call_target="InvertDiagBlocksLowerTriangular" | custom-call | tf_op jit(solution)/shard_map/triangular_solve/custom-call.3 | solution.py:16
  262.2 40.7 %custom-call.38 = f32[4,128,128]{1,2,0:T(8,128)} custom-call(f32[4,128,128]{2,1,0:T(8,128)} %get-tuple-element.48), custom_call_target="InvertDiagBlocksLowerTriangular" | custom-call | tf_op jit(solution)/shard_map/triangular_solve/custom-call.3 | solution.py:16
  314.4 12.3 %collective-permute-done.4 = f32[512,512]{1,0:T(8,128)S(1)} collective-permute-done((f32[512,512]{1,0:T(8,128)S(1)}, f32[512,512]{1,0:T(8,128)S(1)}, u32[]{:S(2)}, u32[]{:S(2)}) %collective-permute-start.4) | collective-permute-done | bytes 1048608 | tf_op jit(solution)/shard_map/ppermute | solution.py:12
  328.6 15.1 %all-gather.13.cloned.1.call-done = f32[512,512]{0,1:T(8,128)} async-done(((f32[128,512]{0,1:T(8,128)}), f32[512,512]{0,1:T(8,128)}) %all-gather.13.cloned.1.call-update) | async-done | bytes 1048592 | tf_op jit(solution)/shard_map/all_gather | solution.py:69
  345.6 11.7 %cholesky.446 = f32[128,128]{1,0:T(8,128)S(1)} custom-call(f32[128,128]{1,0:T(8,128)S(1)} %cholesky.599), custom_call_target="Cholesky" | custom-call | tf_op jit(solution)/shard_map/jit(cholesky)/cholesky | solution.py:72
  368.0 11.7 %cholesky.465 = f32[128,128]{1,0:T(8,128)S(1)} custom-call(f32[128,128]{1,0:T(8,128)S(1)} %cholesky.603), custom_call_target="Cholesky" | custom-call | tf_op jit(solution)/shard_map/jit(cholesky)/cholesky | solution.py:72
  390.4 11.7 %cholesky.486 = f32[128,128]{1,0:T(8,128)S(1)} custom-call(f32[128,128]{1,0:T(8,128)S(1)} %cholesky.608), custom_call_target="Cholesky" | custom-call | tf_op jit(solution)/shard_map/jit(cholesky)/cholesky | solution.py:72
  412.5 11.7 %cholesky.503 = f32[128,128]{1,0:T(8,128)S(1)} custom-call(f32[128,128]{1,0:T(8,128)S(1)} %convolution_subtract_fusion.13), custom_call_target="Cholesky" | custom-call | tf_op jit(solution)/shard_map/jit(cholesky)/cholesky | solution.py:72
  437.3 39.3 %custom-call.42 = f32[4,128,128]{1,2,0:T(8,128)S(1)} custom-call(f32[4,128,128]{2,1,0:T(8,128)S(1)} %get-tuple-element.49), custom_call_target="InvertDiagBlocksLowerTriangular" | custom-call | tf_op jit(solution)/shard_map/triangular_solve/custom-call.3 | solution.py:16
  490.7 15.6 %collective-permute-done.6 = f32[512,512]{1,0:T(8,128)S(1)} collective-permute-done((f32[512,512]{1,0:T(8,128)S(1)}, f32[512,512]{1,0:T(8,128)S(1)}, u32[]{:S(2)}, u32[]{:S(2)}) %collective-permute-start.6) | collective-permute-done | bytes 1048608 | tf_op jit(solution)/shard_map/ppermute | solution.py:12
  517.3 40.7 %custom-call.43 = f32[4,128,128]{1,2,0:T(8,128)} custom-call(f32[4,128,128]{2,1,0:T(8,128)} %get-tuple-element.50), custom_call_target="InvertDiagBlocksLowerTriangular" | custom-call | tf_op jit(solution)/shard_map/triangular_solve/custom-call.3 | solution.py:16
  570.0 23.3 %collective-permute-done.7 = f32[512,512]{1,0:T(8,128)S(1)} collective-permute-done((f32[512,512]{1,0:T(8,128)S(1)}, f32[512,512]{1,0:T(8,128)S(1)}, u32[]{:S(2)}, u32[]{:S(2)}) %collective-permute-start.7) | collective-permute-done | bytes 1048608 | tf_op jit(solution)/shard_map/ppermute | solution.py:12
  601.6 11.7 %cholesky.518 = f32[128,128]{1,0:T(8,128)S(1)} custom-call(f32[128,128]{1,0:T(8,128)S(1)} %cholesky.612), custom_call_target="Cholesky" | custom-call | tf_op jit(solution)/shard_map/jit(cholesky)/cholesky | solution.py:72
  624.0 11.7 %cholesky.537 = f32[128,128]{1,0:T(8,128)S(1)} custom-call(f32[128,128]{1,0:T(8,128)S(1)} %cholesky.616), custom_call_target="Cholesky" | custom-call | tf_op jit(solution)/shard_map/jit(cholesky)/cholesky | solution.py:72
  668.6 12.1 %cholesky.575 = f32[128,128]{1,0:T(8,128)S(1)} custom-call(f32[128,128]{1,0:T(8,128)S(1)} %convolution_subtract_fusion.12), custom_call_target="Cholesky" | custom-call | tf_op jit(solution)/shard_map/jit(cholesky)/cholesky | solution.py:72
  693.9 39.3 %custom-call.47 = f32[4,128,128]{1,2,0:T(8,128)S(1)} custom-call(f32[4,128,128]{2,1,0:T(8,128)S(1)} %get-tuple-element.51), custom_call_target="InvertDiagBlocksLowerTriangular" | custom-call | tf_op jit(solution)/shard_map/triangular_solve/custom-call.3 | solution.py:16
  751.6 59.3 %collective-permute-done.9 = f32[512,512]{1,0:T(8,128)S(1)} collective-permute-done((f32[512,512]{1,0:T(8,128)S(1)}, f32[512,512]{1,0:T(8,128)S(1)}, u32[]{:S(2)}, u32[]{:S(2)}) %collective-permute-start.9) | collective-permute-done | bytes 1048608 | tf_op jit(solution)/shard_map/ppermute | solution.py:12
  822.2 40.7 %custom-call.48 = f32[4,128,128]{1,2,0:T(8,128)} custom-call(f32[4,128,128]{2,1,0:T(8,128)} %get-tuple-element.52), custom_call_target="InvertDiagBlocksLowerTriangular" | custom-call | tf_op jit(solution)/shard_map/triangular_solve/custom-call.3 | solution.py:16
  (308 shorter events, 351.0 us)
Async XLA Ops:
  7.2 57.3 %all-gather.9.cloned.1.call-start = ((), (), s32[]{:S(2)}) async-start(), calls=%async_computation | async-start | bytes 2621440 | tf_op jit(solution)/shard_map/all_gather | solution.py:56
  13.1 9.3 %copy-start.12 = (bf16[1,128,512]{2,1,0:T(8,128)(2,1)S(1)}, bf16[1,128,512]{2,1,0:T(8,128)(2,1)}, u32[]{:S(2)}) copy-start(bf16[1,128,512]{2,1,0:T(8,128)(2,1)} %param.11) | copy-start | bytes 393220
  13.7 50.7 %copy-start.13 = (f32[1,128]{1,0:T(1,128)S(1)}, f32[1,128]{1,0:T(1,128)}, u32[]{:S(2)}) copy-start(f32[1,128]{1,0:T(1,128)} %param.12) | copy-start | bytes 1540
  13.9 7.7 collective-permute-start.1
  22.4 76.8 %all-gather.11.cloned.1.call-start = ((), (), s32[]{:S(2)}) async-start(), calls=%async_computation.1 | async-start | bytes 1310720 | tf_op jit(solution)/shard_map/all_gather | solution.py:69
  22.6 6.3 collective-permute-start
  67.8 164.6 %all-gather.21.cloned.1.call-start = ((), (), s32[]{:S(2)}) async-start(), calls=%async_computation.6 | async-start | bytes 1310720 | tf_op jit(solution)/shard_map/all_gather | solution.py:70
  68.6 275.1 %all-gather.13.cloned.1.call-start = ((), (), s32[]{:S(2)}) async-start(), calls=%async_computation.2 | async-start | bytes 1310720 | tf_op jit(solution)/shard_map/all_gather | solution.py:69
  236.9 14.2 %collective-permute-start.3 = (f32[512,512]{1,0:T(8,128)S(1)}, f32[512,512]{1,0:T(8,128)S(1)}, u32[]{:S(2)}, u32[]{:S(2)}) collective-permute-start(f32[512,512]{1,0:T(8,128)S(1)} %get-tuple-element.110), channel_id=1, source_target_pairs={{4,0},{8,4},{12,8},{16,12},{20,16},{24,20},{28,24},{32,28},{36,32}... | collective-permute-start | bytes 3145736 | tf_op jit(solution)/shard_map/ppermute | solution.py:12
  243.7 64.2 %collective-permute-start.2 = (f32[128,512]{0,1:T(8,128)}, f32[128,512]{0,1:T(8,128)S(1)}, u32[]{:S(2)}, u32[]{:S(2)}) collective-permute-start(f32[128,512]{0,1:T(8,128)} %fusion.103), channel_id=1, source_target_pairs={{0,4},{4,8},{8,12},{12,16},{16,20},{20,24},{24,28},{28,32},{32,36}... | collective-permute-start | bytes 786440 | tf_op jit(solution)/shard_map/ppermute | solution.py:12
  310.5 166.1 %all-gather.15.cloned.1.call-start = ((), (), s32[]{:S(2)}) async-start(), calls=%async_computation.3 | async-start | bytes 1310720 | tf_op jit(solution)/shard_map/all_gather | solution.py:70
  310.6 16.1 %collective-permute-start.4 = (f32[512,512]{1,0:T(8,128)S(1)}, f32[512,512]{1,0:T(8,128)S(1)}, u32[]{:S(2)}, u32[]{:S(2)}) collective-permute-start(f32[512,512]{1,0:T(8,128)S(1)} %pad_maximum_fusion), channel_id=1, source_target_pairs={{4,0},{8,4},{12,8},{16,12},{20,16},{24,20},{28,24},{32,28},{36,32}... | collective-permute-start | bytes 3145736 | tf_op jit(solution)/shard_map/ppermute | solution.py:12
  328.2 271.6 %all-gather.17.cloned.1.call-start = ((), (), s32[]{:S(2)}) async-start(), calls=%async_computation.4 | async-start | bytes 1310720 | tf_op jit(solution)/shard_map/all_gather | solution.py:69
  476.6 6.1 copy-start.1
  480.3 25.9 %collective-permute-start.6 = (f32[512,512]{1,0:T(8,128)S(1)}, f32[512,512]{1,0:T(8,128)S(1)}, u32[]{:S(2)}, u32[]{:S(2)}) collective-permute-start(f32[512,512]{1,0:T(8,128)S(1)} %get-tuple-element.108), channel_id=1, source_target_pairs={{8,0},{12,4},{16,8},{20,12},{24,16},{28,20},{32,24},{36,28},{40,32... | collective-permute-start | bytes 3145736 | tf_op jit(solution)/shard_map/ppermute | solution.py:12
  486.9 77.9 %collective-permute-start.5 = (f32[128,512]{0,1:T(8,128)}, f32[128,512]{0,1:T(8,128)S(1)}, u32[]{:S(2)}, u32[]{:S(2)}) collective-permute-start(f32[128,512]{0,1:T(8,128)} %fusion.101), channel_id=1, source_target_pairs={{0,8},{4,12},{8,16},{12,20},{16,24},{20,28},{24,32},{28,36},{32,40... | collective-permute-start | bytes 786440 | tf_op jit(solution)/shard_map/ppermute | solution.py:12
  558.1 4.2 copy-start.10
  567.3 165.9 %all-gather.19.cloned.1.call-start = ((), (), s32[]{:S(2)}) async-start(), calls=%async_computation.5 | async-start | bytes 1310720 | tf_op jit(solution)/shard_map/all_gather | solution.py:70
  567.4 26.0 %collective-permute-start.7 = (f32[512,512]{1,0:T(8,128)S(1)}, f32[512,512]{1,0:T(8,128)S(1)}, u32[]{:S(2)}, u32[]{:S(2)}) collective-permute-start(f32[512,512]{1,0:T(8,128)S(1)} %pad_maximum_fusion.2), channel_id=1, source_target_pairs={{8,0},{12,4},{16,8},{20,12},{24,16},{28,20},{32,24},{36,28},{40,32... | collective-permute-start | bytes 3145736 | tf_op jit(solution)/shard_map/ppermute | solution.py:12
  733.2 6.1 copy-start
  736.9 74.0 %collective-permute-start.9 = (f32[512,512]{1,0:T(8,128)S(1)}, f32[512,512]{1,0:T(8,128)S(1)}, u32[]{:S(2)}, u32[]{:S(2)}) collective-permute-start(f32[512,512]{1,0:T(8,128)S(1)} %get-tuple-element.106), channel_id=1, source_target_pairs={{16,0},{20,4},{24,8},{28,12},{32,16},{36,20},{40,24},{44,28},{48,3... | collective-permute-start | bytes 3145736 | tf_op jit(solution)/shard_map/ppermute | solution.py:12
  740.9 131.4 %collective-permute-start.10 = (f32[512,512]{1,0:T(8,128)S(1)}, f32[512,512]{1,0:T(8,128)}, u32[]{:S(2)}, u32[]{:S(2)}) collective-permute-start(f32[512,512]{1,0:T(8,128)S(1)} %pad_maximum_fusion.4), channel_id=1, source_target_pairs={{16,0},{20,4},{24,8},{28,12},{32,16},{36,20},{40,24},{44,28},{48,3... | collective-permute-start | bytes 3145736 | tf_op jit(solution)/shard_map/ppermute | solution.py:12
  745.4 124.3 %collective-permute-start.8 = (f32[128,512]{0,1:T(8,128)}, f32[128,512]{0,1:T(8,128)S(1)}, u32[]{:S(2)}, u32[]{:S(2)}) collective-permute-start(f32[128,512]{0,1:T(8,128)} %fusion.99), channel_id=1, source_target_pairs={{0,16},{4,20},{8,24},{12,28},{16,32},{20,36},{24,40},{28,44},{32,4... | collective-permute-start | bytes 786440 | tf_op jit(solution)/shard_map/ppermute | solution.py:12
  862.9 4.2 copy-start.11
  (8 other events, 17.1 us)
Sparse Core Ops, SparseCore 0:
  22.5 41.8 all-gather.8
  67.9 31.2 all-gather.10
  101.9 32.4 all-gather.20
  310.6 33.0 all-gather.12
  346.2 30.5 all-gather.14
  567.5 32.2 all-gather.16
  602.4 30.6 all-gather.18
where the time goes:
time: 894 us; the launch traced here: 882 us
  other arithmetic  487 us (54%)
  waiting for transfers between devices  210 us (23%)
  local copies, waits for them, and re-layouts  64.4 us (7%)
  matrix products  64 us (7%)
  starting transfers between devices  32.1 us (4%)
  between operations  23.4 us (3%)
    another operation x19, other arithmetic, tri_solve(): lax.linalg.triangular_solve(factor, right, left_side=True, lower=True)  242 us
    another operation x45, other arithmetic, shards(): factor = jnp.linalg.cholesky(full_diag)  238 us
    ppermute x11, waiting for transfers between devices, passed_along(): return lax.ppermute(block, axis, route)  124 us
    another operation x79, local copies, waits for them, and re-layouts, tri_solve(): lax.linalg.triangular_solve(factor, right, left_side=True, lower=True)  55.7 us
    all_gather x3, waiting for transfers between devices, shards(): lax.all_gather(diag_rows, 'swath', axis=0, tiled=True)  50.5 us
    all_gather x1, waiting for transfers between devices, shards(): shard_rows = lax.all_gather(gram_input, 'swath', axis=0, tiled=True)  35.5 us
    another operation x42, matrix products, tri_solve(): lax.linalg.triangular_solve(factor, right, left_side=True, lower=True)  35 us
    ppermute x11, starting transfers between devices, passed_along(): return lax.ppermute(block, axis, route)  31.4 us
  transfers between devices with their start and end apart: 18, of which 11 were waited for; matrix products, arithmetic and copies ran while one was open for 66% of the time, Pallas kernels for 0%

commit v1 on v0

--- a/solution.py
+++ b/solution.py
@@ -1,9 +1,33 @@
+import functools
 import jax
 import jax.numpy as jnp
 from jax import lax
 from jax.sharding import PartitionSpec as P
 
 LEVELS = 3
+
+
+def place_the_vector(array_here, across):
+    parts_n = jax.lax.axis_size(across)
+    lanes = []
+    for dev_i in range(parts_n):
+        lanes.append((dev_i, (dev_i + 1) % parts_n))
+    series = []
+    for dev_i in range(parts_n):
+        series.append((dev_i, (dev_i - 1) % parts_n))
+    carry, block_last = ([array_here], [array_here])
+    for _ in range(parts_n // 2):
+        carry.append(jax.lax.ppermute(carry[-1], across, perm=lanes))
+    for _ in range((parts_n - 1) // 2):
+        block_last.append(jax.lax.ppermute(block_last[-1], across, perm=series))
+    near = jnp.concatenate([*carry[::-1], *block_last[1:]], axis=0)
+    tile_out = jnp.roll(
+        near, (jax.lax.axis_index(across) - parts_n // 2) * array_here.shape[0], axis=0
+    )
+    return tile_out
+
+
+make_entries = functools.partial(place_the_vector, across="swath")
 
 
 def passed_along(block, axis, distance):
@@ -53,7 +77,7 @@
     ahead_blocks = compact(scaled, live & (target == my_time + 1), slot_count)
     incoming, previous = passed_along((ahead_blocks, process), "tm", 1)
     gram_input = jnp.concatenate([own_blocks, incoming], axis=0).reshape(-1, order_size)
-    shard_rows = lax.all_gather(gram_input, "swath", axis=0, tiled=True)
+    shard_rows = make_entries(gram_input)
     columns = lax.dynamic_slice_in_dim(shard_rows, row_start, row_count, 1)
     gram = lax.dot_general(
         columns, shard_rows, (((0,), (0,)), ((), ())), preferred_element_type=jnp.float32

time: 894 us -> 826 us (0.924)
  the two profiles are of different devices: /device:TPU:16 before, /device:TPU:48 now
where the time goes in v1:
time: 826 us; the launch traced here: 820 us
  other arithmetic  496 us (60%)
  waiting for transfers between devices  114 us (14%)
  matrix products  75.9 us (9%)
  local copies, waits for them, and re-layouts  65.3 us (8%)
  starting transfers between devices  45.5 us (6%)
  between operations  23.6 us (3%)
    another operation x19, other arithmetic, tri_solve(): lax.linalg.triangular_solve(factor, right, left_side=True, lower=True)  248 us
    another operation x45, other arithmetic, shards(): factor = jnp.linalg.cholesky(full_diag)  238 us
    all_gather x3, waiting for transfers between devices, shards(): lax.all_gather(diag_rows, 'swath', axis=0, tiled=True)  56.6 us
    another operation x79, local copies, waits for them, and re-layouts, tri_solve(): lax.linalg.triangular_solve(factor, right, left_side=True, lower=True)  56.5 us
    another operation x42, matrix products, tri_solve(): lax.linalg.triangular_solve(factor, right, left_side=True, lower=True)  45.5 us
    ppermute x11, waiting for transfers between devices, passed_along(): return lax.ppermute(block, axis, route)  39.5 us
    ppermute x11, starting transfers between devices, passed_along(): return lax.ppermute(block, axis, route)  34.2 us
    dot_general x9, matrix products, inner_rows(): lax.dot_general(left_side, right_side, (((0,), (0,)), ((), ())), precisio...  22.9 us
  transfers between devices with their start and end apart: 20, of which 9 were waited for; matrix products, arithmetic and copies ran while one was open for 75% of the time, Pallas kernels for 0%

profile of v1, /device:TPU:48, one launch (start us, length us, event | category | flops | bytes accessed | tf_op | source)
XLA Modules:
  0.0 820.5 jit_solution(3685771204073556627)
XLA Ops:
  25.0 11.8 %collective-permute-done.2 = bf16[512,512]{1,0:T(8,128)(2,1)S(1)} collective-permute-done((bf16[512,512]{1,0:T(8,128)(2,1)S(1)}, bf16[512,512]{1,0:T(8,128)(2,1)S(1)}, u32[]{:S(2)}, u32[]{:S(2)}) %collective-permute-start.2) | collective-permute-done | bytes 524320 | tf_op jit(solution)/shard_map/ppermute | solution.py:20
  55.8 36.9 %all-gather.8.cloned.1.call-done = f32[512,512]{0,1:T(8,128)} async-done(((f32[128,512]{0,1:T(8,128)}), f32[512,512]{0,1:T(8,128)}) %all-gather.8.cloned.1.call-update) | async-done | bytes 1048592 | tf_op jit(solution)/shard_map/all_gather | solution.py:93
  95.8 11.7 %cholesky.374 = f32[128,128]{1,0:T(8,128)S(1)} custom-call(f32[128,128]{1,0:T(8,128)S(1)} %cholesky.586), custom_call_target="Cholesky" | custom-call | tf_op jit(solution)/shard_map/jit(cholesky)/cholesky | solution.py:96
  118.1 11.7 %cholesky.393 = f32[128,128]{1,0:T(8,128)S(1)} custom-call(f32[128,128]{1,0:T(8,128)S(1)} %cholesky.590), custom_call_target="Cholesky" | custom-call | tf_op jit(solution)/shard_map/jit(cholesky)/cholesky | solution.py:96
  141.8 11.7 %cholesky.414 = f32[128,128]{1,0:T(8,128)S(1)} custom-call(f32[128,128]{1,0:T(8,128)S(1)} %cholesky.595), custom_call_target="Cholesky" | custom-call | tf_op jit(solution)/shard_map/jit(cholesky)/cholesky | solution.py:96
  164.6 11.7 %cholesky.431 = f32[128,128]{1,0:T(8,128)S(1)} custom-call(f32[128,128]{1,0:T(8,128)S(1)} %convolution_subtract_fusion.14), custom_call_target="Cholesky" | custom-call | tf_op jit(solution)/shard_map/jit(cholesky)/cholesky | solution.py:96
  189.9 39.3 %custom-call.37 = f32[4,128,128]{1,2,0:T(8,128)S(1)} custom-call(f32[4,128,128]{2,1,0:T(8,128)S(1)} %get-tuple-element.47), custom_call_target="InvertDiagBlocksLowerTriangular" | custom-call | tf_op jit(solution)/shard_map/triangular_solve/custom-call.3 | solution.py:40
  255.5 40.8 %custom-call.38 = f32[4,128,128]{1,2,0:T(8,128)} custom-call(f32[4,128,128]{2,1,0:T(8,128)} %get-tuple-element.48), custom_call_target="InvertDiagBlocksLowerTriangular" | custom-call | tf_op jit(solution)/shard_map/triangular_solve/custom-call.3 | solution.py:40
  309.6 12.3 %collective-permute-done.7 = f32[512,512]{1,0:T(8,128)S(1)} collective-permute-done((f32[512,512]{1,0:T(8,128)S(1)}, f32[512,512]{1,0:T(8,128)S(1)}, u32[]{:S(2)}, u32[]{:S(2)}) %collective-permute-start.7) | collective-permute-done | bytes 1048608 | tf_op jit(solution)/shard_map/ppermute | solution.py:36
  323.6 15.2 %all-gather.10.cloned.1.call-done = f32[512,512]{0,1:T(8,128)} async-done(((f32[128,512]{0,1:T(8,128)}), f32[512,512]{0,1:T(8,128)}) %all-gather.10.cloned.1.call-update) | async-done | bytes 1048592 | tf_op jit(solution)/shard_map/all_gather | solution.py:93
  341.8 11.7 %cholesky.446 = f32[128,128]{1,0:T(8,128)S(1)} custom-call(f32[128,128]{1,0:T(8,128)S(1)} %cholesky.599), custom_call_target="Cholesky" | custom-call | tf_op jit(solution)/shard_map/jit(cholesky)/cholesky | solution.py:96
  364.2 11.7 %cholesky.465 = f32[128,128]{1,0:T(8,128)S(1)} custom-call(f32[128,128]{1,0:T(8,128)S(1)} %cholesky.603), custom_call_target="Cholesky" | custom-call | tf_op jit(solution)/shard_map/jit(cholesky)/cholesky | solution.py:96
  387.9 11.7 %cholesky.486 = f32[128,128]{1,0:T(8,128)S(1)} custom-call(f32[128,128]{1,0:T(8,128)S(1)} %cholesky.608), custom_call_target="Cholesky" | custom-call | tf_op jit(solution)/shard_map/jit(cholesky)/cholesky | solution.py:96
  410.7 11.7 %cholesky.503 = f32[128,128]{1,0:T(8,128)S(1)} custom-call(f32[128,128]{1,0:T(8,128)S(1)} %convolution_subtract_fusion.13), custom_call_target="Cholesky" | custom-call | tf_op jit(solution)/shard_map/jit(cholesky)/cholesky | solution.py:96
  437.4 39.9 %custom-call.42 = f32[4,128,128]{1,2,0:T(8,128)} custom-call(f32[4,128,128]{2,1,0:T(8,128)S(1)} %get-tuple-element.49), custom_call_target="InvertDiagBlocksLowerTriangular" | custom-call | tf_op jit(solution)/shard_map/triangular_solve/custom-call.3 | solution.py:40
  491.8 10.6 %while.15 = (s32[]{:T(128)}, f32[512,512]{1,0:T(8,128)S(1)}, s32[4,2]{0,1:T(2,128)S(1)}, f32[4,128,128]{2,1,0:T(8,128)}, s32[]{:T(128)}) while((s32[]{:T(128)}, f32[512,512]{1,0:T(8,128)S(1)}, s32[4,2]{0,1:T(2,128)S(1)}, f32[4,128,128]{2,1,0:T(8,128)}, s32[]{:T(128)}) %tuple.157), condition=%wide.while_cond.clone.2, body=%wide.while_body.clone.2.sunk | while | flops 2 | bytes 132705 | solution.py:40
  502.4 40.8 %custom-call.43 = f32[4,128,128]{1,2,0:T(8,128)} custom-call(f32[4,128,128]{2,1,0:T(8,128)} %get-tuple-element.50), custom_call_target="InvertDiagBlocksLowerTriangular" | custom-call | tf_op jit(solution)/shard_map/triangular_solve/custom-call.3 | solution.py:40
  558.6 22.8 %collective-permute-done.10 = f32[512,512]{1,0:T(8,128)S(1)} collective-permute-done((f32[512,512]{1,0:T(8,128)S(1)}, f32[512,512]{1,0:T(8,128)S(1)}, u32[]{:S(2)}, u32[]{:S(2)}) %collective-permute-start.10) | collective-permute-done | bytes 1048608 | tf_op jit(solution)/shard_map/ppermute | solution.py:36
  590.4 11.7 %cholesky.518 = f32[128,128]{1,0:T(8,128)S(1)} custom-call(f32[128,128]{1,0:T(8,128)S(1)} %cholesky.612), custom_call_target="Cholesky" | custom-call | tf_op jit(solution)/shard_map/jit(cholesky)/cholesky | solution.py:96
  612.8 11.7 %cholesky.537 = f32[128,128]{1,0:T(8,128)S(1)} custom-call(f32[128,128]{1,0:T(8,128)S(1)} %cholesky.616), custom_call_target="Cholesky" | custom-call | tf_op jit(solution)/shard_map/jit(cholesky)/cholesky | solution.py:96
  636.7 11.7 %cholesky.558 = f32[128,128]{1,0:T(8,128)S(1)} custom-call(f32[128,128]{1,0:T(8,128)S(1)} %cholesky.621), custom_call_target="Cholesky" | custom-call | tf_op jit(solution)/shard_map/jit(cholesky)/cholesky | solution.py:96
  659.6 11.9 %cholesky.575 = f32[128,128]{1,0:T(8,128)S(1)} custom-call(f32[128,128]{1,0:T(8,128)S(1)} %convolution_subtract_fusion.12), custom_call_target="Cholesky" | custom-call | tf_op jit(solution)/shard_map/jit(cholesky)/cholesky | solution.py:96
  687.1 39.9 %custom-call.47 = f32[4,128,128]{1,2,0:T(8,128)} custom-call(f32[4,128,128]{2,1,0:T(8,128)S(1)} %get-tuple-element.51), custom_call_target="InvertDiagBlocksLowerTriangular" | custom-call | tf_op jit(solution)/shard_map/triangular_solve/custom-call.3 | solution.py:40
  758.0 40.8 %custom-call.48 = f32[4,128,128]{1,2,0:T(8,128)} custom-call(f32[4,128,128]{2,1,0:T(8,128)} %get-tuple-element.52), custom_call_target="InvertDiagBlocksLowerTriangular" | custom-call | tf_op jit(solution)/shard_map/triangular_solve/custom-call.3 | solution.py:40
  (307 shorter events, 359.4 us)
Async XLA Ops:
  7.2 85.6 %all-gather.8.cloned.1.call-start = ((), (), s32[]{:S(2)}) async-start(), calls=%async_computation | async-start | bytes 1310720 | tf_op jit(solution)/shard_map/all_gather | solution.py:93
  13.9 7.7 collective-permute-start.1
  21.6 15.2 %collective-permute-start.2 = (bf16[512,512]{1,0:T(8,128)(2,1)S(1)}, bf16[512,512]{1,0:T(8,128)(2,1)S(1)}, u32[]{:S(2)}, u32[]{:S(2)}) collective-permute-start(bf16[512,512]{1,0:T(8,128)(2,1)S(1)} %bitcast.250), channel_id=1, source_target_pairs={{0,1},{1,2},{2,3},{3,0},{4,5},{5,6},{6,7},{7,4},{8,9},{9,10},{10,1... | collective-permute-start | bytes 1572872 | tf_op jit(solution)/shard_map/ppermute | solution.py:20
  36.9 14.3 %collective-permute-start.3 = (bf16[512,512]{1,0:T(8,128)(2,1)S(1)}, bf16[512,512]{1,0:T(8,128)(2,1)S(1)}, u32[]{:S(2)}, u32[]{:S(2)}) collective-permute-start(bf16[512,512]{1,0:T(8,128)(2,1)S(1)} %collective-permute-done.2), channel_id=1, source_target_pairs={{0,1},{1,2},{2,3},{3,0},{4,5},{5,6},{6,7},{7,4},{8,9},{9,10},{10,1... | collective-permute-start | bytes 1572872 | tf_op jit(solution)/shard_map/ppermute | solution.py:20
  39.0 13.3 %collective-permute-start.4 = (bf16[512,512]{1,0:T(8,128)(2,1)S(1)}, bf16[512,512]{1,0:T(8,128)(2,1)S(1)}, u32[]{:S(2)}, u32[]{:S(2)}) collective-permute-start(bf16[512,512]{1,0:T(8,128)(2,1)S(1)} %bitcast.251), channel_id=1, source_target_pairs={{0,3},{1,0},{2,1},{3,2},{4,7},{5,4},{6,5},{7,6},{8,11},{9,8},{10,9... | collective-permute-start | bytes 1572872 | tf_op jit(solution)/shard_map/ppermute | solution.py:22
  44.0 8.5 %collective-permute-start = (bf16[1,128,512]{1,2,0:T(8,128)(2,1)S(1)}, bf16[1,128,512]{1,2,0:T(8,128)(2,1)S(1)}, u32[]{:S(2)}, u32[]{:S(2)}) collective-permute-start(bf16[1,128,512]{1,2,0:T(8,128)(2,1)S(1)} %copy.20), channel_id=1, source_target_pairs={{0,4},{4,8},{8,12},{12,16},{16,20},{20,24},{24,28},{28,32},{32,36}... | collective-permute-start | bytes 393224 | tf_op jit(solution)/shard_map/ppermute | solution.py:36
  54.5 174.8 %all-gather.18.cloned.1.call-start = ((), (), s32[]{:S(2)}) async-start(), calls=%async_computation.5 | async-start | bytes 1310720 | tf_op jit(solution)/shard_map/all_gather | solution.py:94
  55.3 283.5 %all-gather.10.cloned.1.call-start = ((), (), s32[]{:S(2)}) async-start(), calls=%async_computation.1 | async-start | bytes 1310720 | tf_op jit(solution)/shard_map/all_gather | solution.py:93
  180.1 62.9 %collective-permute-start.6 = (f32[512,512]{1,0:T(8,128)S(1)}, f32[512,512]{1,0:T(8,128)}, u32[]{:S(2)}, u32[]{:S(2)}) collective-permute-start(f32[512,512]{1,0:T(8,128)S(1)} %get-tuple-element.110), channel_id=1, source_target_pairs={{4,0},{8,4},{12,8},{16,12},{20,16},{24,20},{28,24},{32,28},{36,32}... | collective-permute-start | bytes 3145736 | tf_op jit(solution)/shard_map/ppermute | solution.py:36
  235.0 61.2 %copy-start.2 = (f32[1,512,512]{1,2,0:T(8,128)S(1)}, f32[1,512,512]{1,2,0:T(8,128)}, u32[]{:S(2)}) copy-start(f32[1,512,512]{1,2,0:T(8,128)} %all-gather.18.cloned.1.call-done) | copy-start | bytes 3145732
  240.6 62.3 %collective-permute-start.5 = (f32[128,512]{0,1:T(8,128)}, f32[128,512]{0,1:T(8,128)}, u32[]{:S(2)}, u32[]{:S(2)}) collective-permute-start(f32[128,512]{0,1:T(8,128)} %fusion.104), channel_id=1, source_target_pairs={{0,4},{4,8},{8,12},{12,16},{16,20},{20,24},{24,28},{28,32},{32,36}... | collective-permute-start | bytes 786440 | tf_op jit(solution)/shard_map/ppermute | solution.py:36
  255.5 47.4 %copy-start.5 = (f32[128,512]{0,1:T(8,128)S(1)}, f32[128,512]{0,1:T(8,128)}, u32[]{:S(2)}) copy-start(f32[128,512]{0,1:T(8,128)} %fusion.72) | copy-start | bytes 786436
  306.4 171.0 %all-gather.12.cloned.1.call-start = ((), (), s32[]{:S(2)}) async-start(), calls=%async_computation.2 | async-start | bytes 1310720 | tf_op jit(solution)/shard_map/all_gather | solution.py:94
  306.4 15.5 %collective-permute-start.7 = (f32[512,512]{1,0:T(8,128)S(1)}, f32[512,512]{1,0:T(8,128)S(1)}, u32[]{:S(2)}, u32[]{:S(2)}) collective-permute-start(f32[512,512]{1,0:T(8,128)S(1)} %pad_maximum_fusion), channel_id=1, source_target_pairs={{4,0},{8,4},{12,8},{16,12},{20,16},{24,20},{28,24},{32,28},{36,32}... | collective-permute-start | bytes 3145736 | tf_op jit(solution)/shard_map/ppermute | solution.py:36
  323.4 264.0 %all-gather.14.cloned.1.call-start = ((), (), s32[]{:S(2)}) async-start(), calls=%async_computation.3 | async-start | bytes 1310720 | tf_op jit(solution)/shard_map/all_gather | solution.py:93
  426.2 63.5 %collective-permute-start.9 = (f32[512,512]{1,0:T(8,128)S(1)}, f32[512,512]{1,0:T(8,128)}, u32[]{:S(2)}, u32[]{:S(2)}) collective-permute-start(f32[512,512]{1,0:T(8,128)S(1)} %get-tuple-element.108), channel_id=1, source_target_pairs={{8,0},{12,4},{16,8},{20,12},{24,16},{28,20},{32,24},{36,28},{40,32... | collective-permute-start | bytes 3145736 | tf_op jit(solution)/shard_map/ppermute | solution.py:36
  487.0 64.5 %collective-permute-start.8 = (f32[128,512]{0,1:T(8,128)}, f32[128,512]{0,1:T(8,128)}, u32[]{:S(2)}, u32[]{:S(2)}) collective-permute-start(f32[128,512]{0,1:T(8,128)} %fusion.102), channel_id=1, source_target_pairs={{0,8},{4,12},{8,16},{12,20},{16,24},{20,28},{24,32},{28,36},{32,40... | collective-permute-start | bytes 786440 | tf_op jit(solution)/shard_map/ppermute | solution.py:36
  502.4 49.1 %copy-start.4 = (f32[128,512]{0,1:T(8,128)S(1)}, f32[128,512]{0,1:T(8,128)}, u32[]{:S(2)}) copy-start(f32[128,512]{0,1:T(8,128)} %subtract_subtract_fusion.1) | copy-start | bytes 786436
  555.0 172.0 %all-gather.16.cloned.1.call-start = ((), (), s32[]{:S(2)}) async-start(), calls=%async_computation.4 | async-start | bytes 1310720 | tf_op jit(solution)/shard_map/all_gather | solution.py:94
  555.0 26.3 %collective-permute-start.10 = (f32[512,512]{1,0:T(8,128)S(1)}, f32[512,512]{1,0:T(8,128)S(1)}, u32[]{:S(2)}, u32[]{:S(2)}) collective-permute-start(f32[512,512]{1,0:T(8,128)S(1)} %pad_maximum_fusion.2), channel_id=1, source_target_pairs={{8,0},{12,4},{16,8},{20,12},{24,16},{28,20},{32,24},{36,28},{40,32... | collective-permute-start | bytes 3145736 | tf_op jit(solution)/shard_map/ppermute | solution.py:36
  675.0 70.8 %collective-permute-start.12 = (f32[512,512]{1,0:T(8,128)S(1)}, f32[512,512]{1,0:T(8,128)}, u32[]{:S(2)}, u32[]{:S(2)}) collective-permute-start(f32[512,512]{1,0:T(8,128)S(1)} %get-tuple-element.106), channel_id=1, source_target_pairs={{16,0},{20,4},{24,8},{28,12},{32,16},{36,20},{40,24},{44,28},{48,3... | collective-permute-start | bytes 3145736 | tf_op jit(solution)/shard_map/ppermute | solution.py:36
  734.2 76.5 %collective-permute-start.13 = (f32[512,512]{1,0:T(8,128)S(1)}, f32[512,512]{1,0:T(8,128)}, u32[]{:S(2)}, u32[]{:S(2)}) collective-permute-start(f32[512,512]{1,0:T(8,128)S(1)} %pad_maximum_fusion.4), channel_id=1, source_target_pairs={{16,0},{20,4},{24,8},{28,12},{32,16},{36,20},{40,24},{44,28},{48,3... | collective-permute-start | bytes 3145736 | tf_op jit(solution)/shard_map/ppermute | solution.py:36
  739.1 67.9 %collective-permute-start.11 = (f32[128,512]{0,1:T(8,128)}, f32[128,512]{0,1:T(8,128)}, u32[]{:S(2)}, u32[]{:S(2)}) collective-permute-start(f32[128,512]{0,1:T(8,128)} %fusion.100), channel_id=1, source_target_pairs={{0,16},{4,20},{8,24},{12,28},{16,32},{20,36},{24,40},{28,44},{32,4... | collective-permute-start | bytes 786440 | tf_op jit(solution)/shard_map/ppermute | solution.py:36
  758.0 49.1 %copy-start.3 = (f32[128,512]{0,1:T(8,128)S(1)}, f32[128,512]{0,1:T(8,128)}, u32[]{:S(2)}) copy-start(f32[128,512]{0,1:T(8,128)} %subtract_subtract_fusion) | copy-start | bytes 786436
  (4 other events, 54.9 us)
Sparse Core Ops, SparseCore 0:
  54.6 38.1 all-gather.7
  95.4 31.9 all-gather.17
  306.5 32.2 all-gather.9
  341.3 30.7 all-gather.11
  555.1 32.2 all-gather.13
  589.9 30.7 all-gather.15
